TPU v7x, 32 devices: a whole 2x2x4 slice. The times are simulated.
32 devices in a mesh: group: 2 (over x), ep: 16 (over z, y, core).
Axes of the slice: x: 2, y: 2, z: 4, core: 2. Of those that a mesh axis runs over, the one named last changes fastest.
Arguments:
- tokens: bfloat16 [4096, 4096], P(('group', 'ep')), parts along dimension 0, may hold values from -6 to 6
- expert_ids: int32 [4096, 8], P(('group', 'ep')), parts along dimension 0, may hold values from 0 to 15, all different within a row; in each aligned block of 128 rows (0 to 127, 128 to 255, ...) at most 80 rows name the same one
- route_weights: bfloat16 [4096, 8], P(('group', 'ep')), parts along dimension 0, may hold values from 0.049804688 to 1
- smooth: float32 [4096], replicated, may hold values from 0.3 to 3
- gate_weight: bfloat16 [16, 4096, 768], P('ep'), may hold values from -0.09375 to 0.09375
- up_weight: bfloat16 [16, 4096, 768], P('ep'), may hold values from -0.09375 to 0.09375
- down_weight: bfloat16 [16, 768, 4096], P('ep'), may hold values from -0.21875 to 0.21875
Outputs:
- mixed: bfloat16 [4096, 4096], P(('group', 'ep')), parts along dimension 0
There are 2 independent parts, one for each index of `group`. A program takes and returns all parts, laid end to end along the dimension named above; an argument that names none is the same for every part. Nothing has to cross between parts.
Inputs may be any that keep to these rules, and one draw needn't show every extreme that they name: `expert_ids`: A row's 8 ids are distinct. In each aligned block of 128 rows (the rows of one device) no expert is named by more than 80 rows, a bound that some block reaches.
All inputs are finite; a program needn't handle non-finite values.
Results may differ from a plain program's by a relative error of at most 0.007.
Values may be sent and summed in bfloat16 or wider, within the bound.
A program may use at most 128 MiB of HBM per device.

v0:
```python
import jax
import jax.numpy as jnp
from jax import lax
from jax.sharding import PartitionSpec as P


def expert_rows(rows, folded_gate, folded_up, down_one):
    gate = jnp.dot(rows, folded_gate, preferred_element_type=jnp.float32)
    upper = jnp.dot(rows, folded_up, preferred_element_type=jnp.float32)
    hidden = (jax.nn.silu(gate) * upper).astype(jnp.bfloat16)
    return jnp.dot(hidden, down_one, preferred_element_type=jnp.float32).astype(jnp.bfloat16)


def shards(tokens, expert_ids, route_weights, smooth, gate_weight, up_weight, down_weight):
    tok_dev, topk = expert_ids.shape
    width = tokens.shape[1]
    experts = lax.axis_size("ep")
    capacity = 5 * tok_dev * topk // (4 * experts)
    folded_gate = (smooth[:, None] * gate_weight[0].astype(jnp.float32)).astype(jnp.bfloat16)
    folded_up = (smooth[:, None] * up_weight[0].astype(jnp.float32)).astype(jnp.bfloat16)
    down_one = down_weight[0]
    flat_ids = expert_ids.reshape(-1)
    onehot = (flat_ids[:, None] == jnp.arange(experts, dtype=jnp.int32)[None, :]).astype(jnp.int32)
    before = jnp.cumsum(onehot, axis=0) - onehot
    slot = jnp.sum(before * onehot, axis=1)
    target = flat_ids * capacity + slot
    outgoing = jnp.zeros((experts * capacity, width), jnp.bfloat16)
    outgoing = outgoing.at[target].set(jnp.repeat(tokens, topk, axis=0))
    outgoing = outgoing.reshape(experts, capacity, width)
    arrived = lax.all_to_all(outgoing, "ep", split_axis=0, concat_axis=0, tiled=True)
    result = expert_rows(arrived.reshape(-1, width), folded_gate, folded_up, down_one)
    returned = lax.all_to_all(
        result.reshape(arrived.shape), "ep", split_axis=0, concat_axis=0, tiled=True
    )
    gathered = jnp.take(returned.reshape(experts * capacity, width), target, axis=0)
    gathered = gathered.reshape(tok_dev, topk, width)
    mixed = jnp.einsum("tk,tkd->td", route_weights, gathered, preferred_element_type=jnp.float32)
    return mixed.astype(jnp.bfloat16)


def solution(mesh):
    placed = (
        P(("group", "ep"), None),
        P(("group", "ep"), None),
        P(("group", "ep"), None),
        P(),
        P("ep", None, None),
        P("ep", None, None),
        P("ep", None, None),
    )
    return jax.shard_map(
        shards, mesh=mesh, in_specs=placed, out_specs=P(("group", "ep"), None), check_vma=False
    )
```

profile of v0, /device:TPU:15, one launch (start us, length us, event | category | flops | bytes accessed | tf_op | source)
XLA Modules:
  0.0 556.2 jit_solution(17285631600146173208)
XLA Ops:
  0.0 0.0 copy-start
  0.0 0.9 copy.16
  0.9 0.1 eq.26
  1.0 0.1 reshape.89
  1.1 0.7 broadcast_multiply_fusion
  1.8 4.5 reduce-window.6
  6.3 0.1 slice.10
  6.4 0.1 copy.18
  6.5 0.1 copy.19
  6.6 0.1 broadcast_add_fusion
  6.7 0.1 copy.22
  6.8 0.1 mul.48
  6.9 0.0 copy-done
  7.0 17.2 %scatter_custom_fusion = bf16[1280,4096]{1,0:T(8,128)(2,1)} fusion(s32[1024]{0:T(1024)S(1)} %bitcast.58, bf16[]{:T(256)} %constant.27.clone.1, bf16[128,4096]{1,0:T(8,128)(2,1)S(1)} %copy-done), kind=kCustom, calls=%fused_computation.7 | custom fusion | bytes 11534338 | tf_op jit(solution)/shard_map/scatter | solution.py:28
  24.1 0.0 copy-start.4
  24.1 0.0 slice-start
  24.2 233.9 %all_to_all.10 = bf16[16,80,4096]{2,1,0:T(8,128)(2,1)S(1)} all-to-all(bf16[16,80,4096]{2,1,0:T(8,128)(2,1)} %bitcast.51), channel_id=1, replica_groups=mesh['group'=2,'ep'=16] {'ep'}, dimensions={0} | all-to-all | bytes 20971520 | tf_op jit(solution)/shard_map/all_to_all | solution.py:30
  258.0 0.0 copy-done.4
  258.0 0.0 slice-start.1
  258.0 12.2 %fusion.5 = f32[1280,768]{1,0:T(8,128)} fusion(bf16[1280,4096]{1,0:T(8,128)(2,1)S(1)} %bitcast.53, bf16[1,4096,768]{2,1,0:T(8,128)(2,1)} %param.11, f32[4096]{0:T(1024)S(1)} %copy-done.4), kind=kOutput, calls=%fused_computation.11 | convolution fusion | flops 8062500864 | bytes 20725760 | tf_op jit(solution)/shard_map/dot_general | solution.py:8
  270.2 0.0 slice-done
  270.2 0.0 slice-done.1
  270.2 10.7 %fusion.19 = bf16[1280,768]{1,0:T(8,128)(2,1)S(1)} fusion(bf16[1280,4096]{1,0:T(8,128)(2,1)S(1)} %bitcast.54, bf16[1,4096,768]{2,1,0:T(8,128)(2,1)S(1)} %bitcast.62, f32[4096]{0:T(1024)S(1)} %copy-done.4, f32[1280,768]{1,0:T(8,128)} %fusion.5), kind=kOutput, calls=%fused_computation.21 | convolution fusion | flops 8068399104 | bytes 22691840 | tf_op jit(solution)/shard_map/dot_general | solution.py:9
  280.9 13.4 %convolution_convert_fusion = bf16[1280,4096]{1,0:T(8,128)(2,1)} fusion(bf16[1280,768]{1,0:T(8,128)(2,1)S(1)} %fusion.19, bf16[1,768,4096]{2,1,0:T(8,128)(2,1)} %param.13), kind=kOutput, calls=%fused_computation.2 | convolution fusion | flops 8058306560 | bytes 18743296 | tf_op jit(solution)/shard_map/dot_general | solution.py:11
  294.4 0.0 copy-start.2
  294.4 0.0 copy-start.3
  294.4 6.1 %all-to-all-start.1 = ((bf16[16,80,4096]{2,1,0:T(8,128)(2,1)}), bf16[16,80,4096]{2,1,0:T(8,128)(2,1)}, u32[]{:S(2)}, u32[]{:S(2)}) async-start(bf16[16,80,4096]{2,1,0:T(8,128)(2,1)} %bitcast.52), calls=%async_computation.1 | async-start | bytes 20971520 | tf_op jit(solution)/shard_map/all_to_all | solution.py:32
  300.4 0.1 reduce_sum.14
  300.6 0.0 copy-done.2
  300.6 0.1 copy.21
  300.7 0.0 copy-done.3
  300.7 0.1 copy.23
  300.9 226.8 %all-to-all-done.1 = bf16[16,80,4096]{2,1,0:T(8,128)(2,1)} async-done(((bf16[16,80,4096]{2,1,0:T(8,128)(2,1)}), bf16[16,80,4096]{2,1,0:T(8,128)(2,1)}, u32[]{:S(2)}, u32[]{:S(2)}) %all-to-all-start.1) | async-done | bytes 10485792 | tf_op jit(solution)/shard_map/all_to_all | solution.py:32
  527.7 0.0 copy-start.1
  527.7 20.5 %gather_fusion = bf16[1024,4096]{1,0:T(8,128)(2,1)} fusion(bf16[1280,4096]{1,0:T(8,128)(2,1)} %bitcast.11, s32[1024]{0:T(1024)S(1)} %broadcast_clamp_fusion), kind=kCustom, calls=%fused_computation | custom fusion | bytes 16781312 | tf_op jit(solution)/shard_map/jit(_take)/gather | solution.py:35
  548.3 5.8 %fusion = bf16[128,1,4096]{2,1,0:T(2,128)(2,1)S(1)} fusion(bf16[128,8,1]{1,2,0:T(2,128)(2,1)S(1)} %copy.23, bf16[1024,4096]{1,0:T(8,128)(2,1)} %gather_fusion, pred[128,8]{1,0:T(8,128)(4,1)S(1)} %copy.21), kind=kOutput, calls=%fused_computation.6 | convolution fusion | flops 12582912 | bytes 9440256 | tf_op jit(solution)/shard_map/tk,tkd->td/dot_general | solution.py:37
  554.1 2.1 copy.28
  556.2 0.0 copy-done.1
  (9 shorter events, 0.2 us)
Async XLA Ops:
  0.0 7.0 %copy-start = (bf16[128,4096]{1,0:T(8,128)(2,1)S(1)}, bf16[128,4096]{1,0:T(8,128)(2,1)}, u32[]{:S(2)}) copy-start(bf16[128,4096]{1,0:T(8,128)(2,1)} %param.7) | copy-start | bytes 3145732
  24.1 233.9 %copy-start.4 = (f32[4096]{0:T(1024)S(1)}, f32[4096]{0:T(1024)}, u32[]{:S(2)}) copy-start(f32[4096]{0:T(1024)} %param.10) | copy-start | bytes 49156
  24.1 246.1 %slice-start = ((s8[6291456]{0:T(1024)(128)(4,1)}), s8[4194304]{0:T(1024)(128)(4,1)S(1)}, s32[]{:S(2)}) async-start(s8[6291456]{0:T(1024)(128)(4,1)} %bitcast.61), calls=%async_computation.2 | async-start | bytes 8388608
  258.0 12.2 %slice-start.1 = ((s8[6291456]{0:T(1024)(128)(4,1)}), s8[2097152]{0:T(1024)(128)(4,1)S(1)}, s32[]{:S(2)}) async-start(s8[6291456]{0:T(1024)(128)(4,1)} %bitcast.61), calls=%async_computation.3 | async-start | bytes 4194304
  294.4 6.2 %copy-start.2 = (s32[128,8]{0,1:T(8,128)S(1)}, s32[128,8]{0,1:T(8,128)}, u32[]{:S(2)}) copy-start(s32[128,8]{0,1:T(8,128)} %param.8) | copy-start | bytes 12292
  294.4 6.4 %copy-start.3 = (bf16[128,8]{0,1:T(8,128)(2,1)S(1)}, bf16[128,8]{0,1:T(8,128)(2,1)}, u32[]{:S(2)}) copy-start(bf16[128,8]{0,1:T(8,128)(2,1)} %param.9) | copy-start | bytes 6148
  294.4 233.4 %all-to-all-start.1 = ((bf16[16,80,4096]{2,1,0:T(8,128)(2,1)}), bf16[16,80,4096]{2,1,0:T(8,128)(2,1)}, u32[]{:S(2)}, u32[]{:S(2)}) async-start(bf16[16,80,4096]{2,1,0:T(8,128)(2,1)} %bitcast.52), calls=%async_computation.1 | async-start | bytes 20971520 | tf_op jit(solution)/shard_map/all_to_all | solution.py:32
  527.7 28.5 %copy-start.1 = (bf16[128,4096]{1,0:T(8,128)(2,1)S(1)}, bf16[128,4096]{1,0:T(8,128)(2,1)}, u32[]{:S(2)}) copy-start(bf16[128,4096]{1,0:T(8,128)(2,1)} %param.7) | copy-start | bytes 3145732
where the time goes:
time: 557 us; the launch traced here: 556 us
  blocking collectives  234 us (42%)
  waiting for transfers between devices  227 us (41%)
  matrix products  42.1 us (8%)
  local copies, waits for them, and re-layouts  41.8 us (8%)
  starting transfers between devices  6.06 us (1%)
    all_to_all x1, blocking collectives, shards(): lax.all_to_all(outgoing, 'ep', split_axis=0, concat_axis=0, tiled=True)  234 us
    all_to_all x1, waiting for transfers between devices, shards(): lax.all_to_all(result.reshape(arrived.shape), 'ep', split_axis=0, concat_...  227 us
    gather x1, local copies, waits for them, and re-layouts, shards(): jnp.take(returned.reshape(experts * capacity, width), target, axis=0)  20.5 us
    scatter x1, local copies, waits for them, and re-layouts, shards(): outgoing = outgoing.at[target].set(jnp.repeat(tokens, topk, axis=0))  17.2 us
    dot_general x1, matrix products, expert_rows(): jnp.dot(hidden, down_one, preferred_element_type=jnp.float32)  13.4 us
    dot_general x1, matrix products, expert_rows(): gate = jnp.dot(rows, folded_gate, preferred_element_type=jnp.float32)  12.2 us
  transfers between devices with their start and end apart: 1, of which 1 were waited for; matrix products, arithmetic and copies ran while one was open for 0% of the time, Pallas kernels for 0%

commit v1 on v0

v1 whole, which is shorter than its diff:
```python
import jax
import jax.numpy as jnp
from jax import lax
from jax.sharding import PartitionSpec as P

CHUNKS = 2


def shards(tokens, expert_ids, route_weights, smooth, gate_weight, up_weight, down_weight):
    tok_dev, topk = expert_ids.shape
    width = tokens.shape[1]
    experts = lax.axis_size("ep")
    me = lax.axis_index("ep")
    rows = tok_dev // CHUNKS
    chosen = expert_ids[:, :, None] == jnp.arange(experts, dtype=jnp.int32)[None, None, :]
    spread = jnp.sum(
        jnp.where(chosen, route_weights[:, :, None].astype(jnp.float32), 0.0), axis=1
    ).astype(jnp.bfloat16)
    spread_all = lax.all_gather(spread, "ep", axis=0, tiled=False)
    mine = lax.dynamic_slice_in_dim(spread_all, me, 1, axis=2).astype(jnp.float32)
    gathered = [
        lax.all_gather(tokens[i * rows : (i + 1) * rows], "ep", axis=0, tiled=True)
        for i in range(CHUNKS)
    ]
    folded_gate = (smooth[:, None] * gate_weight[0].astype(jnp.float32)).astype(jnp.bfloat16)
    folded_up = (smooth[:, None] * up_weight[0].astype(jnp.float32)).astype(jnp.bfloat16)
    down_one = down_weight[0]
    outs = []
    for i in range(CHUNKS):
        gate = jnp.dot(gathered[i], folded_gate, preferred_element_type=jnp.float32)
        upper = jnp.dot(gathered[i], folded_up, preferred_element_type=jnp.float32)
        hidden = (jax.nn.silu(gate) * upper).astype(jnp.bfloat16)
        result = jnp.dot(hidden, down_one, preferred_element_type=jnp.float32)
        scale = mine[:, i * rows : (i + 1) * rows].reshape(experts * rows, 1)
        part = (result * scale).astype(jnp.bfloat16)
        outs.append(lax.psum_scatter(part, "ep", scatter_dimension=0, tiled=True))
    return jnp.concatenate(outs, axis=0)


def solution(mesh):
    placed = (
        P(("group", "ep"), None),
        P(("group", "ep"), None),
        P(("group", "ep"), None),
        P(),
        P("ep", None, None),
        P("ep", None, None),
        P("ep", None, None),
    )
    return jax.shard_map(
        shards, mesh=mesh, in_specs=placed, out_specs=P(("group", "ep"), None), check_vma=False
    )
```

time: 557 us -> 387 us (0.69)
  the two profiles are of different devices: /device:TPU:15 before, /device:TPU:0 now
where the time goes in v1:
time: 387 us
  waiting for transfers between devices  274 us (71%)
  matrix products  69.2 us (18%)
  blocking collectives  23.7 us (6%)
  between operations  13.2 us (3%)
    reduce_scatter x2, waiting for transfers between devices, shards(): outs.append(lax.psum_scatter(part, 'ep', scatter_dimension=0, tiled=True))  180 us
    all_gather x2, waiting for transfers between devices, shards(): lax.all_gather(tokens[i * rows:(i + 1) * rows], 'ep', axis=0, tiled=True)  93.2 us
    dot_general x2, matrix products, shards(): gate = jnp.dot(gathered[i], folded_gate, preferred_element_type=jnp.float32)  27.2 us
    all_gather x1, blocking collectives, shards(): spread_all = lax.all_gather(spread, 'ep', axis=0, tiled=False)  23.7 us
    dot_general x2, matrix products, shards(): upper = jnp.dot(gathered[i], folded_up, preferred_element_type=jnp.float32)  23.3 us
    dot_general x2, matrix products, shards(): result = jnp.dot(hidden, down_one, preferred_element_type=jnp.float32)  18.6 us
  transfers between devices with their start and end apart: 4, of which 4 were waited for; matrix products, arithmetic and copies ran while one was open for 18% of the time, Pallas kernels for 0%

profile of v1, /device:TPU:0, one launch (start us, length us, event | category | flops | bytes accessed | tf_op | source)
XLA Modules:
  0.0 386.7 jit_solution(9676083841339701238)
XLA Ops:
  6.5 0.0 all-gather.4.cloned.1.call-start
  6.5 2.3 fusion.24
  8.8 0.0 all-gather.4.cloned.1.call-update
  8.8 0.0 all-gather.6.cloned.1.call-start
  8.9 0.7 all-gather.6.cloned.1.call-update
  9.6 0.0 reduce-scatter.3.cloned.1.call-start
  9.6 0.7 convert_element_type.57
  10.3 0.7 select_reduce_fusion
  11.0 23.7 %all-gather = bf16[2048,16]{0,1:T(8,128)(2,1)S(1)} all-gather(bf16[128,16]{0,1:T(8,128)(2,1)S(1)} %select_reduce_fusion), channel_id=2, replica_groups=mesh['group'=2,'ep'=16] {'ep'}, dimensions={0}, use_global_device_ids=true | all-gather | bytes 69632 | tf_op jit(solution)/shard_map/all_gather | solution.py:19
  34.8 0.1 fusion.25
  34.8 0.1 mul.52
  34.9 0.0 copy-start.2
  34.9 52.4 %all-gather.4.cloned.1.call-done = bf16[1024,4096]{1,0:T(8,128)(2,1)} async-done(((bf16[64,4096]{1,0:T(8,128)(2,1)}), bf16[1024,4096]{1,0:T(8,128)(2,1)}) %all-gather.4.cloned.1.call-update) | async-done | bytes 8388624 | tf_op jit(solution)/shard_map/all_gather | solution.py:22
  87.3 0.0 copy-start.1
  87.3 0.0 slice-start
  87.3 13.6 %fusion.14 = f32[768,1024]{1,0:T(8,128)} fusion(bf16[1024,4096]{1,0:T(8,128)(2,1)} %all-gather.4.cloned.1.call-done, bf16[1,4096,768]{2,1,0:T(8,128)(2,1)} %param.11, f32[4096]{0:T(1024)} %param.10), kind=kOutput, calls=%fused_computation.23 | convolution fusion | flops 6451888128 | bytes 17842176 | tf_op jit(solution)/shard_map/dot_general | solution.py:30
  100.9 0.0 copy-done.2
  100.9 0.0 copy-done.1
  100.9 0.0 slice-start.1
  100.9 11.5 %fusion.8 = bf16[1024,768]{0,1:T(8,128)(2,1)S(1)} fusion(f32[768,1024]{1,0:T(8,128)} %fusion.14, bf16[1024,4096]{1,0:T(8,128)(2,1)S(1)} %copy-done.1, bf16[1,4096,768]{2,1,0:T(8,128)(2,1)} %param.12, f32[4096]{0:T(1024)S(1)} %copy-done.2), kind=kOutput, calls=%fused_computation.16 | convolution fusion | flops 6456606720 | bytes 19415040 | tf_op jit(solution)/shard_map/dot_general | solution.py:31
  112.4 0.0 slice-done
  112.4 0.0 slice-done.1
  112.4 9.3 %multiply_convert_fusion.1 = bf16[1024,4096]{1,0:T(8,128)(2,1)} fusion(f32[1024]{0:T(1024)S(1)} %mul.52, bf16[1024,768]{0,1:T(8,128)(2,1)S(1)} %fusion.8, bf16[1,768,4096]{2,1,0:T(8,128)(2,1)S(1)} %bitcast.70), kind=kOutput, calls=%fused_computation.1 | convolution fusion | flops 6450839552 | bytes 16257024 | tf_op jit(solution)/shard_map/dot_general | solution.py:33
  121.7 0.0 reduce-scatter.3.cloned.1.call-update
  121.7 0.0 reduce-scatter.5.cloned.1.call-start
  121.8 0.1 mul.57
  121.8 40.8 %all-gather.6.cloned.1.call-done = bf16[1024,4096]{1,0:T(8,128)(2,1)} async-done(((bf16[64,4096]{1,0:T(8,128)(2,1)}), bf16[1024,4096]{1,0:T(8,128)(2,1)}) %all-gather.6.cloned.1.call-update) | async-done | bytes 8388624 | tf_op jit(solution)/shard_map/all_gather | solution.py:22
  162.6 0.0 copy-start
  162.6 0.0 slice-start.2
  162.6 13.6 %fusion.12 = f32[768,1024]{1,0:T(8,128)} fusion(bf16[1024,4096]{1,0:T(8,128)(2,1)} %all-gather.6.cloned.1.call-done, bf16[1,4096,768]{2,1,0:T(8,128)(2,1)} %param.11, f32[4096]{0:T(1024)S(1)} %copy-done.2), kind=kOutput, calls=%fused_computation.22 | convolution fusion | flops 6451888128 | bytes 17842176 | tf_op jit(solution)/shard_map/dot_general | solution.py:30
  176.2 0.0 copy-done
  176.2 0.0 slice-start.3
  176.2 11.9 %fusion.4 = bf16[1024,768]{0,1:T(8,128)(2,1)S(1)} fusion(f32[768,1024]{1,0:T(8,128)} %fusion.12, bf16[1024,4096]{1,0:T(8,128)(2,1)S(1)} %copy-done, bf16[1,4096,768]{2,1,0:T(8,128)(2,1)} %param.12, f32[4096]{0:T(1024)S(1)} %copy-done.2), kind=kOutput, calls=%fused_computation.9 | convolution fusion | flops 6456606720 | bytes 19415040 | tf_op jit(solution)/shard_map/dot_general | solution.py:31
  188.1 0.0 slice-done.2
  188.1 0.0 slice-done.3
  188.2 9.4 %multiply_convert_fusion = bf16[1024,4096]{1,0:T(8,128)(2,1)} fusion(f32[1024]{0:T(1024)S(1)} %mul.57, bf16[1024,768]{0,1:T(8,128)(2,1)S(1)} %fusion.4, bf16[1,768,4096]{2,1,0:T(8,128)(2,1)S(1)} %bitcast.72), kind=kOutput, calls=%fused_computation | convolution fusion | flops 6450839552 | bytes 16257024 | tf_op jit(solution)/shard_map/dot_general | solution.py:33
  197.5 0.0 reduce-scatter.5.cloned.1.call-update
  197.5 72.0 %reduce-scatter.3.cloned.1.call-done = bf16[64,4096]{1,0:T(8,128)(2,1)} async-done(((bf16[1024,4096]{1,0:T(8,128)(2,1)}), bf16[64,4096]{1,0:T(8,128)(2,1)}) %reduce-scatter.3.cloned.1.call-update) | async-done | bytes 524304 | tf_op jit(solution)/shard_map/reduce_scatter | solution.py:36
  269.6 108.3 %reduce-scatter.5.cloned.1.call-done = bf16[64,4096]{1,0:T(8,128)(2,1)} async-done(((bf16[1024,4096]{1,0:T(8,128)(2,1)}), bf16[64,4096]{1,0:T(8,128)(2,1)}) %reduce-scatter.5.cloned.1.call-update) | async-done | bytes 524304 | tf_op jit(solution)/shard_map/reduce_scatter | solution.py:36
  377.9 2.3 pad_maximum_fusion
  (4 shorter events, 0.0 us)
Async XLA Ops:
  6.5 80.7 %all-gather.4.cloned.1.call-start = ((), (), s32[]{:S(2)}) async-start(), calls=%async_computation.2 | async-start | bytes 8912896 | tf_op jit(solution)/shard_map/all_gather | solution.py:22
  8.8 153.8 %all-gather.6.cloned.1.call-start = ((), (), s32[]{:S(2)}) async-start(), calls=%async_computation.4 | async-start | bytes 8912896 | tf_op jit(solution)/shard_map/all_gather | solution.py:22
  9.6 260.0 %reduce-scatter.3.cloned.1.call-start = ((), (), s32[]{:S(2)}) async-start(), calls=%async_computation.3 | async-start | bytes 8912896 | tf_op jit(solution)/shard_map/reduce_scatter | solution.py:36
  34.9 66.0 %copy-start.2 = (f32[4096]{0:T(1024)S(1)}, f32[4096]{0:T(1024)}, u32[]{:S(2)}) copy-start(f32[4096]{0:T(1024)} %param.10) | copy-start | bytes 49156
  87.3 13.6 %copy-start.1 = (bf16[1024,4096]{1,0:T(8,128)(2,1)S(1)}, bf16[1024,4096]{1,0:T(8,128)(2,1)}, u32[]{:S(2)}) copy-start(bf16[1024,4096]{1,0:T(8,128)(2,1)} %all-gather.4.cloned.1.call-done) | copy-start | bytes 25165828
  87.3 25.1 %slice-start = ((s8[6291456]{0:T(1024)(128)(4,1)}), s8[4194304]{0:T(1024)(128)(4,1)S(1)}, s32[]{:S(2)}) async-start(s8[6291456]{0:T(1024)(128)(4,1)} %bitcast.69), calls=%async_computation.6 | async-start | bytes 8388608
  100.9 11.5 %slice-start.1 = ((s8[6291456]{0:T(1024)(128)(4,1)}), s8[2097152]{0:T(1024)(128)(4,1)S(1)}, s32[]{:S(2)}) async-start(s8[6291456]{0:T(1024)(128)(4,1)} %bitcast.69), calls=%async_computation.7 | async-start | bytes 4194304
  121.7 256.2 %reduce-scatter.5.cloned.1.call-start = ((), (), s32[]{:S(2)}) async-start(), calls=%async_computation.5 | async-start | bytes 8912896 | tf_op jit(solution)/shard_map/reduce_scatter | solution.py:36
  162.6 13.6 %copy-start = (bf16[1024,4096]{1,0:T(8,128)(2,1)S(1)}, bf16[1024,4096]{1,0:T(8,128)(2,1)}, u32[]{:S(2)}) copy-start(bf16[1024,4096]{1,0:T(8,128)(2,1)} %all-gather.6.cloned.1.call-done) | copy-start | bytes 25165828
  162.6 25.5 %slice-start.2 = ((s8[6291456]{0:T(1024)(128)(4,1)}), s8[4194304]{0:T(1024)(128)(4,1)S(1)}, s32[]{:S(2)}) async-start(s8[6291456]{0:T(1024)(128)(4,1)} %bitcast.71), calls=%async_computation.8 | async-start | bytes 8388608
  176.2 11.9 %slice-start.3 = ((s8[6291456]{0:T(1024)(128)(4,1)}), s8[2097152]{0:T(1024)(128)(4,1)S(1)}, s32[]{:S(2)}) async-start(s8[6291456]{0:T(1024)(128)(4,1)} %bitcast.71), calls=%async_computation.9 | async-start | bytes 4194304
Sparse Core Ops, SparseCore 0:
  9.5 77.7 all-gather.3
  89.4 73.1 all-gather.5
  166.7 102.8 reduce-scatter.2
  273.5 104.3 reduce-scatter.4
